TPU v7x, 32 devices: a whole 2x2x4 slice. The times are simulated.
32 devices in a mesh: inst: 4 (over z), circ: 4 (over x, core), ax: 2 (over y).
Axes of the slice: x: 2, y: 2, z: 4, core: 2. Of those that a mesh axis runs over, the one named last changes fastest.
Arguments:
- state_start: float32 [16, 5, 64, 16, 512], P('inst', None, 'ax', None, 'circ'), may hold values from -6 to 6
- forcing: float32 [16, 5, 64, 16, 512], P('inst', None, 'ax', None, 'circ'), may hold values from -6 to 6
- pseudo_step: float32 [64, 16, 512], P('ax', None, 'circ'), may hold values from 0.1 to 0.4
- flux_jacobians: float32 [3, 5, 5], replicated, may hold values from -3 to 3
- interp_weights: float32 [16, 128, 128], P('inst'), may hold values from -0.5 to 0.5
- sector_shift: int32 [16], P('inst'), may hold values from 0 to 3
Outputs:
- state_final: float32 [16, 5, 64, 16, 512], P('inst', None, 'ax', None, 'circ')
- last_residual: float32 [16, 5, 64, 16, 512], P('inst', None, 'ax', None, 'circ')
Inputs may be any that keep to these rules, and one draw needn't show every extreme that they name: `sector_shift`: the rotor's sector offset of an instance.
All inputs are finite; a program needn't handle non-finite values.
Results may differ from a plain program's by a relative error of at most 0.0001.
Values sent between devices are 32-bit elements; how exact they have to be, the bound alone decides.
A program may use at most 256 MiB of HBM per device.

v0:
```python
import jax
import jax.numpy as jnp
from jax import lax
from jax.sharding import PartitionSpec as P

ITERS = 2


FREQUENCY = 0.25
SMOOTHING = 0.25


def from_partner(array, axis, stride):
    return lax.ppermute(array, axis, [(i, i ^ 1 << stride) for i in range(lax.axis_size(axis))])


def from_behind(block, axis, distance):
    devices = range(lax.axis_size(axis))
    route = [((i - distance) % len(devices), i) for i in devices]
    return lax.ppermute(block, axis, route)


def with_halo(cells, sides, width):
    for axis, dim in sides:
        count = lax.axis_size(axis)
        head = lax.slice_in_dim(cells, 0, width, axis=dim)
        tail = lax.slice_in_dim(cells, cells.shape[dim] - width, cells.shape[dim], axis=dim)
        cells = jnp.concatenate(
            [
                lax.ppermute(tail, axis, [(i, (i + 1) % count) for i in range(count)]),
                cells,
                lax.ppermute(head, axis, [((i + 1) % count, i) for i in range(count)]),
            ],
            axis=dim,
        )
    return cells


def spectral_table(count):
    order = jnp.arange(count, dtype=jnp.int32)
    offsets = order[:, None] - order[None, :]
    safe_gap = jnp.where(offsets == 0, 1, offsets)
    parity = (1 - 2 * jnp.mod(offsets, 2)).astype(jnp.float32)
    angles = jnp.pi * safe_gap.astype(jnp.float32) / count
    entries = 0.5 * FREQUENCY * parity * jnp.cos(angles) / jnp.sin(angles)
    return jnp.where(offsets == 0, 0.0, entries)


def directional(jacobian, field, before, after):
    central = (after - before) * 0.5
    second = after - 2.0 * field + before
    moved = jnp.einsum("vw,iwarc->ivarc", jacobian, central, precision=lax.Precision.HIGHEST)
    return moved - SMOOTHING * second


def local(state_start, forcing, pseudo_step, flux_jacobians, interp_weights, sector_shift):
    local_count = state_start.shape[0]
    spectral = spectral_table(local_count * lax.axis_size("inst"))
    own_rows = lax.dynamic_slice_in_dim(
        spectral, lax.axis_index("inst") * local_count, local_count, 0
    )
    axial_side = lax.axis_index("ax")
    cycle_size = lax.axis_size("circ")
    turn_count = jnp.where(
        axial_side == 1, sector_shift, jnp.mod(cycle_size - sector_shift, cycle_size)
    )
    blend_weights = jnp.where(axial_side == 1, interp_weights, jnp.swapaxes(interp_weights, 1, 2))
    state = state_start
    zero_radial = jnp.zeros_like(state[:, :, :, :1])
    last_residual = state
    for step in range(ITERS):
        boundary = jnp.where(axial_side == 0, state[:, :, -1], state[:, :, 0])
        partner = from_partner(boundary, "ax", 0)
        for bit_number in range(cycle_size.bit_length() - 1):
            moved_rows = from_behind(partner, "circ", 1 << bit_number)
            taken_mask = jnp.mod(turn_count // (1 << bit_number), 2) == 1
            partner = jnp.where(taken_mask[:, None, None, None], moved_rows, partner)
        ghost_row = jnp.einsum(
            "ivrq,itq->ivrt", partner, blend_weights, precision=lax.Precision.HIGHEST
        )
        zero_face = jnp.zeros_like(ghost_row)
        after_axial = jnp.concatenate(
            [state[:, :, 1:], jnp.where(axial_side == 0, ghost_row, zero_face)[:, :, None]], axis=2
        )
        before_axial = jnp.concatenate(
            [jnp.where(axial_side == 1, ghost_row, zero_face)[:, :, None], state[:, :, :-1]], axis=2
        )
        after_radial = jnp.concatenate([state[:, :, :, 1:], zero_radial], axis=3)
        before_radial = jnp.concatenate([zero_radial, state[:, :, :, :-1]], axis=3)
        padded = with_halo(state, (("circ", 4),), 1)
        before_tangent = padded[..., :-2]
        after_tangent = padded[..., 2:]
        flux = directional(flux_jacobians[0], state, before_axial, after_axial)
        flux = flux + directional(flux_jacobians[1], state, before_radial, after_radial)
        flux = flux + directional(flux_jacobians[2], state, before_tangent, after_tangent)
        coupled = jnp.einsum(
            "nm,mvarc->nvarc",
            own_rows,
            lax.all_gather(state, "inst", axis=0, tiled=True),
            precision=lax.Precision.HIGHEST,
        )
        last_residual = flux + coupled - forcing
        state = state - pseudo_step[None, None] * last_residual
    return (state, last_residual)


def solution(mesh):
    placed = (
        P("inst", None, "ax", None, "circ"),
        P("inst", None, "ax", None, "circ"),
        P("ax", None, "circ"),
        P(),
        P("inst", None, None),
        P("inst"),
    )
    return jax.shard_map(
        local,
        mesh=mesh,
        in_specs=placed,
        out_specs=(P("inst", None, "ax", None, "circ"), P("inst", None, "ax", None, "circ")),
        check_vma=False,
    )
```

profile of v0, /device:TPU:8, one launch (start us, length us, event | category | flops | bytes accessed | tf_op | source)
XLA Modules:
  0.0 895.7 jit_solution(13867409926803973848)
XLA Ops:
  7.2 0.7 all-gather.3.cloned.1.call-update
  8.0 1.0 fusion.93
  9.0 0.1 fusion.47
  9.1 1.6 collective-permute-start
  10.7 11.0 %fusion.92 = (f32[4,5,32,16,1]{4,3,2,1,0:T(8,128)}, f32[4,5,32,16,1]{4,3,2,1,0:T(8,128)}) fusion(f32[4,5,32,16,128]{4,3,2,1,0:T(8,128)} %param.6), kind=kLoop, calls=%fused_computation.136 | loop fusion | bytes 163840 | tf_op jit(solution)/shard_map/slice | solution.py:27
  21.7 4.6 copy.86
  26.3 0.3 collective-permute-start.3
  26.6 4.1 copy.87
  30.7 0.8 collective-permute-start.4
  31.5 9.4 %copy.62 = f32[4,5,32,16,128]{4,1,3,2,0:T(8,128)} copy(f32[4,5,32,16,128]{4,3,2,1,0:T(8,128)} %param.6) | data formatting | bytes 10485760 | tf_op args[0]
  41.0 12.2 %fusion.91 = (f32[4,5,32,15,128]{4,1,3,2,0:T(8,128)}, f32[4,5,32,15,128]{4,1,3,2,0:T(8,128)}) fusion(f32[4,5,32,16,128]{4,1,3,2,0:T(8,128)} %copy.62), kind=kLoop, calls=%fused_computation.135 | loop fusion | bytes 19660800 | tf_op jit(solution)/shard_map/slice | solution.py:88
  53.2 13.4 %fusion.26 = f32[4,32,16,128,5]{3,4,2,1,0:T(8,128)} fusion(f32[4,5,32,15,128]{4,1,3,2,0:T(8,128)} %get-tuple-element.17, f32[4,5,32,15,128]{4,1,3,2,0:T(8,128)} %get-tuple-element.16, f32[1,5,5]{2,0,1:T(1,128)S(1)} %get-tuple-element.27), kind=kOutput, calls=%fused_computation.44 | convolution fusion | flops 81264640 | bytes 15073380 | tf_op jit(solution)/shard_map/vw,iwarc->ivarc/dot_general | solution.py:52
  66.6 6.7 fusion.90
  73.3 1.1 collective-permute-start.1
  74.5 4.9 collective-permute-done.1
  79.4 0.1 broadcast_select_fusion.1
  79.5 1.6 collective-permute-start.2
  81.1 0.1 copy.42
  81.2 7.6 copy.56
  88.8 7.6 copy.54
  96.3 0.1 broadcast_select_fusion.3
  96.4 0.6 select_bitcast_fusion.3
  97.2 13.9 %fusion.29 = f32[4,32,16,128,5]{3,4,2,1,0:T(8,128)} fusion(f32[4,5,31,16,128]{4,1,3,2,0:T(8,128)} %get-tuple-element.15, f32[4,5,1,16,128]{4,1,3,2,0:T(8,128)S(1)} %copy.46, f32[4,5,1,16,128]{4,1,3,2,0:T(8,128)S(1)} %copy.44, f32[4,5,31,16,128]{4,1,3,2,0:T(8,128)} %get-tuple-element.14, f32[1,5,5]{2,0,1:T(1,128)S(1)} %get-tuple-element.28), kind=kOutput, calls=%fused_computation.47 | convolution fusion | flops 83886080 | bytes 15728740 | tf_op jit(solution)/shard_map/vw,iwarc->ivarc/dot_general | solution.py:52
  111.1 253.9 %all-gather.3.cloned.1.call-done = f32[16,5,32,16,128]{4,3,2,1,0:T(8,128)} async-done(((f32[4,5,32,16,128]{4,3,2,1,0:T(8,128)}), f32[16,5,32,16,128]{4,3,2,1,0:T(8,128)}) %all-gather.3.cloned.1.call-update) | async-done | bytes 20971536 | tf_op jit(solution)/shard_map/all_gather | solution.py:99
  365.0 25.5 %fusion.2 = f32[4,5,32,16,128]{4,0,3,2,1:T(4,128)} fusion(f32[16,5,32,16,128]{4,3,2,1,0:T(8,128)} %all-gather.3.cloned.1.call-done, s32[16,16]{1,0:T(8,128)S(1)} %get-tuple-element.32, s32[]{:T(128)S(6)} %select_n.131, s32[16,16]{1,0:T(8,128)S(1)} %get-tuple-element.31, pred[16,16]{1,0:T(8,128)(4,1)S(1)} %fusion.57), kind=kOutput, calls=%fused_computation.2 | convolution fusion | flops 251658752 | bytes 26219012 | tf_op jit(solution)/shard_map/nm,mvarc->nvarc/dot_general | solution.py:96
  390.6 48.6 %fusion.5 = f32[4,5,32,16,128]{4,1,3,2,0:T(8,128)} fusion(f32[4,5,32,16,128]{4,1,3,2,0:T(8,128)} %copy.62, f32[4,5,32,16,128]{4,3,2,1,0:T(8,128)} %param.7, f32[4,32,16,128,5]{3,4,2,1,0:T(8,128)} %fusion.26, f32[4,32,16,128,5]{3,4,2,1,0:T(8,128)} %fusion.29, f32[4,5,32,16,128]{4,0,3,2,1:T(4,128)} %fusion.2, f32[4,5,32,15,128]{4,1,3,2,0:T(8,128)} %get-tuple-element.17, ...), kind=kOutput, calls=%fused_computation.7 | convolution fusion | flops 114032640 | bytes 52117604 | tf_op jit(solution)/shard_map/vw,iwarc->ivarc/dot_general | solution.py:52
  439.2 6.7 copy.71
  445.9 1.2 fusion.46
  447.1 1.8 collective-permute-start.5
  448.9 15.2 %fusion.87 = (f32[4,5,32,16,1]{4,1,3,2,0:T(8,128)}, f32[4,5,32,16,1]{4,1,3,2,0:T(8,128)}) fusion(f32[4,5,32,16,128]{4,1,3,2,0:T(8,128)} %fusion.5), kind=kLoop, calls=%fused_computation.131 | loop fusion | bytes 163840 | tf_op jit(solution)/shard_map/slice | solution.py:27
  464.1 7.0 fusion.88
  471.1 12.2 %fusion.89 = (f32[4,5,32,15,128]{4,1,3,2,0:T(8,128)}, f32[4,5,32,15,128]{4,1,3,2,0:T(8,128)}) fusion(f32[4,5,32,16,128]{4,1,3,2,0:T(8,128)} %fusion.5), kind=kLoop, calls=%fused_computation.133 | loop fusion | bytes 19660800 | tf_op jit(solution)/shard_map/slice | solution.py:88
  483.3 5.4 copy.69
  488.7 5.3 copy.67
  494.0 1.8 collective-permute-start.8
  495.8 0.1 broadcast_select_fusion
  495.9 1.6 collective-permute-start.7
  497.5 13.4 %fusion.15 = f32[4,32,16,128,5]{3,4,2,1,0:T(8,128)} fusion(f32[4,5,32,15,128]{4,1,3,2,0:T(8,128)} %get-tuple-element.13, f32[4,5,32,15,128]{4,1,3,2,0:T(8,128)} %get-tuple-element.12, f32[1,5,5]{2,0,1:T(1,128)S(1)} %get-tuple-element.27), kind=kOutput, calls=%fused_computation.32 | convolution fusion | flops 81264640 | bytes 15073380 | tf_op jit(solution)/shard_map/vw,iwarc->ivarc/dot_general | solution.py:52
  510.9 7.6 copy.70
  518.5 7.6 copy.68
  526.1 0.1 broadcast_select_fusion.2
  526.2 0.6 select_bitcast_fusion.1
  526.9 13.9 %fusion.18 = f32[4,32,16,128,5]{3,4,2,1,0:T(8,128)} fusion(f32[4,5,31,16,128]{4,1,3,2,0:T(8,128)} %get-tuple-element.11, f32[4,5,1,16,128]{4,1,3,2,0:T(8,128)S(1)} %copy.66, f32[4,5,1,16,128]{4,1,3,2,0:T(8,128)S(1)} %copy.65, f32[4,5,31,16,128]{4,1,3,2,0:T(8,128)} %get-tuple-element.10, f32[1,5,5]{2,0,1:T(1,128)S(1)} %get-tuple-element.28), kind=kOutput, calls=%fused_computation.35 | convolution fusion | flops 83886080 | bytes 15728740 | tf_op jit(solution)/shard_map/vw,iwarc->ivarc/dot_general | solution.py:52
  540.8 260.6 %all-gather.5.cloned.1.call-done = f32[16,5,32,16,128]{4,3,2,1,0:T(8,128)} async-done(((f32[4,5,32,16,128]{4,3,2,1,0:T(8,128)}), f32[16,5,32,16,128]{4,3,2,1,0:T(8,128)}) %all-gather.5.cloned.1.call-update) | async-done | bytes 20971536 | tf_op jit(solution)/shard_map/all_gather | solution.py:99
  801.5 25.5 %fusion = f32[4,5,32,16,128]{4,0,3,2,1:T(4,128)} fusion(f32[16,5,32,16,128]{4,3,2,1,0:T(8,128)} %all-gather.5.cloned.1.call-done, s32[16,16]{1,0:T(8,128)S(1)} %get-tuple-element.32, s32[]{:T(128)S(6)} %select_n.131, s32[16,16]{1,0:T(8,128)S(1)} %get-tuple-element.31, pred[16,16]{1,0:T(8,128)(4,1)S(1)} %fusion.57), kind=kOutput, calls=%fused_computation | convolution fusion | flops 251658752 | bytes 26219012 | tf_op jit(solution)/shard_map/nm,mvarc->nvarc/dot_general | solution.py:96
  827.0 51.5 %multiply_subtract_fusion = (f32[4,5,32,16,128]{4,1,3,2,0:T(8,128)}, f32[4,5,32,16,128]{4,1,3,2,0:T(8,128)}) fusion(f32[4,5,32,16,128]{4,1,3,2,0:T(8,128)} %fusion.5, f32[32,16,128]{2,1,0:T(8,128)S(1)} %copy-done.1, f32[4,5,32,16,128]{4,3,2,1,0:T(8,128)} %param.7, f32[4,5,32,16,128]{4,0,3,2,1:T(4,128)} %fusion, f32[4,5,32,16,1]{4,1,3,2,0:T(8,128)} %copy.70, ...), kind=kOutput, calls=%fused_computation.28 | convolution fusion | flops 114032640 | bytes 57360484 | tf_op jit(solution)/shard_map/vw,iwarc->ivarc/dot_general | solution.py:52
  878.5 6.8 copy.75
  885.3 3.3 copy.76
  (43 shorter events, 0.5 us)
Async XLA Ops:
  7.2 357.9 %all-gather.3.cloned.1.call-start = ((), (), s32[]{:S(2)}) async-start(), calls=%async_computation | async-start | bytes 26214400 | tf_op jit(solution)/shard_map/all_gather | solution.py:99
  7.9 793.6 %all-gather.5.cloned.1.call-start = ((), (), s32[]{:S(2)}) async-start(), calls=%async_computation.1 | async-start | bytes 26214400 | tf_op jit(solution)/shard_map/all_gather | solution.py:99
  9.1 64.2 %collective-permute-start = (f32[4,5,16,128]{3,1,2,0:T(8,128)S(1)}, f32[4,5,16,128]{3,1,2,0:T(8,128)S(1)}, u32[]{:S(2)}, u32[]{:S(2)}) collective-permute-start(f32[4,5,16,128]{3,1,2,0:T(8,128)S(1)} %fusion.47), channel_id=1, source_target_pairs={{0,1},{1,0},{2,3},{3,2},{4,5},{5,4},{6,7},{7,6},{8,9},{9,8},{10,11... | collective-permute-start | bytes 491528 | tf_op jit(solution)/shard_map/ppermute | solution.py:14
  26.3 62.5 %collective-permute-start.3 = (f32[4,5,32,16,1]{2,3,4,1,0:T(8,128)S(1)}, f32[4,5,32,16,1]{2,3,4,1,0:T(8,128)S(1)}, u32[]{:S(2)}, u32[]{:S(2)}) collective-permute-start(f32[4,5,32,16,1]{2,3,4,1,0:T(8,128)S(1)} %copy.86), channel_id=1, source_target_pairs={{2,0},{4,2},{6,4},{0,6},{3,1},{5,3},{7,5},{1,7},{10,8},{12,10},{14... | collective-permute-start | bytes 122888 | tf_op jit(solution)/shard_map/ppermute | solution.py:32
  26.6 14.4 %copy-start.3 = (f32[3,5,5]{2,0,1:T(4,128)S(1)}, f32[3,5,5]{2,0,1:T(4,128)}, u32[]{:S(2)}) copy-start(f32[3,5,5]{2,0,1:T(4,128)} %param.9) | copy-start | bytes 904
  30.7 50.5 %collective-permute-start.4 = (f32[4,5,32,16,1]{2,3,4,1,0:T(8,128)S(1)}, f32[4,5,32,16,1]{2,3,4,1,0:T(8,128)S(1)}, u32[]{:S(2)}, u32[]{:S(2)}) collective-permute-start(f32[4,5,32,16,1]{2,3,4,1,0:T(8,128)S(1)} %copy.87), channel_id=1, source_target_pairs={{0,2},{2,4},{4,6},{6,0},{1,3},{3,5},{5,7},{7,1},{8,10},{10,12},{12... | collective-permute-start | bytes 122888 | tf_op jit(solution)/shard_map/ppermute | solution.py:30
  53.2 13.4 %slice-start.2 = ((s8[8388608]{0:T(1024)(128)(4,1)}), s8[4194304]{0:T(1024)(128)(4,1)S(1)}, s32[]{:S(2)}) async-start(s8[8388608]{0:T(1024)(128)(4,1)} %bitcast.113), calls=%async_computation.4 | async-start | bytes 8388608
  53.2 13.4 %slice-start.3 = ((s8[8388608]{0:T(1024)(128)(4,1)}), s8[4194304]{0:T(1024)(128)(4,1)S(1)}, s32[]{:S(2)}) async-start(s8[8388608]{0:T(1024)(128)(4,1)} %bitcast.113), calls=%async_computation.5 | async-start | bytes 8388608
  66.6 6.7 copy-start.4
  66.6 14.4 %copy-start.2 = (f32[4,128,128]{2,1,0:T(8,128)S(1)}, f32[4,128,128]{2,1,0:T(8,128)}, u32[]{:S(2)}) copy-start(f32[4,128,128]{2,1,0:T(8,128)} %param.10) | copy-start | bytes 786436
  73.3 6.0 collective-permute-start.1
  79.5 16.9 %collective-permute-start.2 = (f32[4,5,16,128]{3,1,2,0:T(8,128)S(1)}, f32[4,5,16,128]{3,1,2,0:T(8,128)S(1)}, u32[]{:S(2)}, u32[]{:S(2)}) collective-permute-start(f32[4,5,16,128]{3,1,2,0:T(8,128)S(1)} %broadcast_select_fusion.1), channel_id=1, source_target_pairs={{4,0},{6,2},{0,4},{2,6},{5,1},{7,3},{1,5},{3,7},{12,8},{14,10},{8,... | collective-permute-start | bytes 491528 | tf_op jit(solution)/shard_map/ppermute | solution.py:20
  365.0 25.5 %copy-start.1 = (f32[32,16,128]{2,1,0:T(8,128)S(1)}, f32[32,16,128]{2,1,0:T(8,128)}, u32[]{:S(2)}) copy-start(f32[32,16,128]{2,1,0:T(8,128)} %param.8) | copy-start | bytes 786436
  445.9 18.2 %slice-start = ((s8[8388608]{0:T(1024)(128)(4,1)}), s8[4194304]{0:T(1024)(128)(4,1)S(1)}, s32[]{:S(2)}) async-start(s8[8388608]{0:T(1024)(128)(4,1)} %bitcast.111), calls=%async_computation.2 | async-start | bytes 8388608
  447.1 17.0 %slice-start.1 = ((s8[8388608]{0:T(1024)(128)(4,1)}), s8[4194304]{0:T(1024)(128)(4,1)S(1)}, s32[]{:S(2)}) async-start(s8[8388608]{0:T(1024)(128)(4,1)} %bitcast.111), calls=%async_computation.3 | async-start | bytes 8388608
  447.1 24.0 %collective-permute-start.5 = (f32[4,5,16,128]{3,1,2,0:T(8,128)S(1)}, f32[4,5,16,128]{3,1,2,0:T(8,128)S(1)}, u32[]{:S(2)}, u32[]{:S(2)}) collective-permute-start(f32[4,5,16,128]{3,1,2,0:T(8,128)S(1)} %fusion.46), channel_id=1, source_target_pairs={{0,1},{1,0},{2,3},{3,2},{4,5},{5,4},{6,7},{7,6},{8,9},{9,8},{10,11... | collective-permute-start | bytes 491528 | tf_op jit(solution)/shard_map/ppermute | solution.py:14
  471.1 24.7 %collective-permute-start.6 = (f32[4,5,16,128]{3,1,2,0:T(8,128)S(1)}, f32[4,5,16,128]{3,1,2,0:T(8,128)S(1)}, u32[]{:S(2)}, u32[]{:S(2)}) collective-permute-start(f32[4,5,16,128]{3,1,2,0:T(8,128)S(1)} %collective-permute-done.5), channel_id=1, source_target_pairs={{6,0},{0,2},{2,4},{4,6},{7,1},{1,3},{3,5},{5,7},{14,8},{8,10},{10,... | collective-permute-start | bytes 491528 | tf_op jit(solution)/shard_map/ppermute | solution.py:20
  494.0 24.5 %collective-permute-start.8 = (f32[4,5,32,16,1]{2,3,4,1,0:T(8,128)S(1)}, f32[4,5,32,16,1]{2,3,4,1,0:T(8,128)S(1)}, u32[]{:S(2)}, u32[]{:S(2)}) collective-permute-start(f32[4,5,32,16,1]{2,3,4,1,0:T(8,128)S(1)} %copy.67), channel_id=1, source_target_pairs={{2,0},{4,2},{6,4},{0,6},{3,1},{5,3},{7,5},{1,7},{10,8},{12,10},{14... | collective-permute-start | bytes 122888 | tf_op jit(solution)/shard_map/ppermute | solution.py:32
  495.8 15.1 %collective-permute-start.9 = (f32[4,5,32,16,1]{2,3,4,1,0:T(8,128)S(1)}, f32[4,5,32,16,1]{2,3,4,1,0:T(8,128)S(1)}, u32[]{:S(2)}, u32[]{:S(2)}) collective-permute-start(f32[4,5,32,16,1]{2,3,4,1,0:T(8,128)S(1)} %copy.69), channel_id=1, source_target_pairs={{0,2},{2,4},{4,6},{6,0},{1,3},{3,5},{5,7},{7,1},{8,10},{10,12},{12... | collective-permute-start | bytes 122888 | tf_op jit(solution)/shard_map/ppermute | solution.py:30
  495.9 30.2 %collective-permute-start.7 = (f32[4,5,16,128]{3,1,2,0:T(8,128)S(1)}, f32[4,5,16,128]{3,1,2,0:T(8,128)S(1)}, u32[]{:S(2)}, u32[]{:S(2)}) collective-permute-start(f32[4,5,16,128]{3,1,2,0:T(8,128)S(1)} %broadcast_select_fusion), channel_id=1, source_target_pairs={{4,0},{6,2},{0,4},{2,6},{5,1},{7,3},{1,5},{3,7},{12,8},{14,10},{8,... | collective-permute-start | bytes 491528 | tf_op jit(solution)/shard_map/ppermute | solution.py:20
  878.4 6.8 copy-start
Sparse Core Ops, SparseCore 0:
  9.6 355.3 all-gather.2
  446.0 355.4 all-gather.4
where the time goes:
time: 903 us; the launch traced here: 896 us
  waiting for transfers between devices  520 us (58%)
  matrix products  207 us (23%)
  local copies, waits for them, and re-layouts  142 us (16%)
  between operations  14.5 us (2%)
  starting transfers between devices  10.7 us (1%)
    all_gather x2, waiting for transfers between devices, local(): lax.all_gather(state, 'inst', axis=0, tiled=True)  515 us
    dot_general x6, matrix products, directional(): jnp.einsum('vw,iwarc->ivarc', jacobian, central, precision=lax.Precision....  155 us
    dot_general x2, matrix products, local(): jnp.einsum('nm,mvarc->nvarc', own_rows, lax.all_gather(state, 'inst', axi...  51.1 us
    slice x3, local copies, waits for them, and re-layouts, with_halo(): lax.slice_in_dim(cells, cells.shape[dim] - width, cells.shape[dim], axis=...  31.5 us
    unnamed x24, local copies, waits for them, and re-layouts  28.4 us
    slice x2, local copies, waits for them, and re-layouts, local(): after_radial = jnp.concatenate([state[:, :, :, 1:], zero_radial], axis=3)  24.5 us
  transfers between devices with their start and end apart: 12, of which 3 were waited for; matrix products, arithmetic and copies ran while one was open for 20% of the time, Pallas kernels for 0%

commit v1 on v0

v1 whole, which is shorter than its diff:
```python
import functools
import math

import jax
import jax.numpy as jnp
from jax import lax
from jax.experimental import pallas as pl
from jax.experimental.pallas import tpu as pltpu
from jax.sharding import PartitionSpec as P

FREQUENCY = 0.25
SMOOTHING = 0.25
MESH = pl.DeviceIdType.MESH
HIGHEST = lax.Precision.HIGHEST
MOST_CHUNKS = 4


def derivative(values):
    count = len(values)
    half = count // 2
    factors = {
        k: 0.5 * FREQUENCY * (-1) ** k / math.tan(math.pi * k / count) for k in range(1, half)
    }
    low, high = [], []
    for n in range(half):
        gaps = {k: values[(n - k) % count] - values[(n + k) % count] for k in range(1, half)}
        first, second = None, None
        for k in range(1, half):
            one, two = factors[k] * gaps[k], factors[k] * gaps[half - k]
            first = one if first is None else first + one
            second = -two if second is None else second - two
        low.append(first)
        high.append(second)
    return low + high


def kernel(
    sizes,
    start_ref, forcing_ref, step_ref, jac_ref, weights_ref, turn_ref,
    final_ref, residual_ref,
    state, force, drive, all_state, all_drive, back, coupled, coupled_next,
    faces, edges, edges_in,
    z_send, z_recv, z_local, f_send, f_recv, e_send, e_recv, load_sem, out_sem,
):
    parts, cycle, chunks = sizes
    instances, comps, layers, radial, width = drive.shape
    total = all_state.shape[0]
    owned = layers // parts
    depth = owned // chunks
    me = lax.axis_index("inst")
    sector = lax.axis_index("circ")
    row = lax.axis_index("ax")

    def other(offset):
        return lax.rem(me + offset, parts)

    def at_sector(offset):
        return lax.rem(sector + offset, cycle)

    barrier = pltpu.get_barrier_semaphore()
    for p in range(1, parts):
        pl.semaphore_signal(barrier, inc=1, device_id={"inst": other(p)}, device_id_type=MESH)
    for p in range(cycle):
        pl.semaphore_signal(
            barrier, inc=1, device_id={"circ": at_sector(p), "ax": 1 - row}, device_id_type=MESH
        )
    for p in (1, cycle - 1):
        pl.semaphore_signal(barrier, inc=1, device_id={"circ": at_sector(p)}, device_id_type=MESH)
    pl.semaphore_wait(barrier, parts - 1 + cycle + 2)

    def face_copy(turn, p):
        layer = (1 - row) * (layers - 1)
        source = start_ref.at[:, :, layer] if turn == 0 else state.at[:, :, layer + 1]
        return pltpu.make_async_remote_copy(
            src_ref=source, dst_ref=faces.at[turn, p],
            send_sem=f_send.at[turn, p], recv_sem=f_recv.at[turn, p],
            device_id={"circ": at_sector(p), "ax": 1 - row}, device_id_type=MESH,
        )

    def edge_copy(turn, side):
        return pltpu.make_async_remote_copy(
            src_ref=edges.at[turn], dst_ref=edges_in.at[turn, side],
            send_sem=e_send.at[turn, side], recv_sem=e_recv.at[turn, side],
            device_id={"circ": at_sector(1 if side == 0 else cycle - 1)}, device_id_type=MESH,
        )

    def out_ends(phase, k, target):
        source = start_ref if phase == 0 else drive
        there = all_state if phase == 0 else all_drive
        return (
            source.at[:, :, pl.ds(target * owned + k * depth, depth)],
            there.at[pl.ds(me * instances, instances), :, pl.ds(k * depth, depth)],
        )

    def back_ends(phase, k, target):
        source = back if phase == 2 else all_state
        there = coupled if phase == 2 else coupled_next
        return (
            source.at[pl.ds(target * instances, instances), :, pl.ds(k * depth, depth)],
            there.at[:, :, pl.ds(me * owned + k * depth, depth)],
        )

    def moves(phase, k):
        ends = out_ends if phase < 2 else back_ends
        found = []
        for p in range(1, parts):
            source, there = ends(phase, k, other(p))
            found.append(
                pltpu.make_async_remote_copy(
                    src_ref=source, dst_ref=there,
                    send_sem=z_send.at[phase, k, p - 1], recv_sem=z_recv.at[phase, k, p - 1],
                    device_id={"inst": other(p)}, device_id_type=MESH,
                )
            )
        return found

    def kept(phase, k):
        source, there = (out_ends if phase < 2 else back_ends)(phase, k, me)
        return pltpu.make_async_copy(source, there, z_local.at[phase, k])

    def begin(phase, k):
        for copy in moves(phase, k):
            copy.start()
        kept(phase, k).start()

    def arrived(phase, k):
        for copy in moves(phase, k):
            copy.wait_recv()
        kept(phase, k).wait()

    def sent(phase):
        for k in range(chunks):
            for copy in moves(phase, k):
                copy.wait_send()

    lane = lax.broadcasted_iota(jnp.int32, (radial, width), 1)
    line = lax.broadcasted_iota(jnp.int32, (radial, width), 0)

    def exchange(turn):
        for p in range(cycle):
            if turn == 1:
                face_copy(turn, p).start()

        def pack(i, carry):
            n, v = i // comps, i % comps
            packed = jnp.zeros((radial, width), jnp.float32)
            for a in range(layers):
                cells = state[n, v, a + 1]
                packed = jnp.where(lane == a, pltpu.roll(cells, a + 1, 1), packed)
                packed = jnp.where(lane == layers + a, pltpu.roll(cells, layers + a, 1), packed)
            edges[turn, n, v] = packed
            return carry

        lax.fori_loop(0, instances * comps, pack, 0)
        for side in range(2):
            edge_copy(turn, side).start()
        for p in range(cycle):
            face_copy(turn, p).wait_recv()
        for n in range(instances):
            taken = jnp.full((comps, radial, width), turn_ref[n], jnp.int32)
            facing = faces[turn, 0, n]
            for p in range(1, cycle):
                facing = jnp.where(taken == p, faces[turn, p, n], facing)
            ghost = jnp.dot(
                facing.reshape(comps * radial, width), weights_ref[n],
                precision=HIGHEST, preferred_element_type=jnp.float32,
            ).reshape(comps, radial, width)
            empty = jnp.zeros_like(ghost)
            state[n, :, 0] = jnp.where(row == 1, ghost, empty)
            state[n, :, layers + 1] = jnp.where(row == 0, ghost, empty)
        for side in range(2):
            edge_copy(turn, side).wait_recv()

    def flux(turn):
        def one(i, carry):
            n, a = i // layers, i % layers
            rises, curves, cells = [[], [], []], [], []
            for w in range(comps):
                cell = state[n, w, a + 1]
                before, after = state[n, w, a], state[n, w, a + 2]
                down = jnp.where(line == 0, 0.0, pltpu.roll(cell, 1, 0))
                up = jnp.where(line == radial - 1, 0.0, pltpu.roll(cell, radial - 1, 0))
                left = pltpu.roll(edges_in[turn, 0, n, w], lax.rem(width - a, width), 1)
                left = jnp.where(lane == 0, left, pltpu.roll(cell, 1, 1))
                right = pltpu.roll(edges_in[turn, 1, n, w], width - 1 - layers - a, 1)
                right = jnp.where(lane == width - 1, right, pltpu.roll(cell, width - 1, 1))
                rises[0].append(after - before)
                rises[1].append(up - down)
                rises[2].append(right - left)
                around = ((after + before) + (up + down)) + (right + left)
                curves.append(SMOOTHING * (6.0 * cell - around))
            for v in range(comps):
                value = curves[v] - force[n, v, a]
                for d in range(3):
                    for w in range(comps):
                        value = value + jac_ref[(d * comps + v) * comps + w] * rises[d][w]
                drive[n, v, a] = value
            return carry

        lax.fori_loop(0, instances * layers, one, 0)

    def couple(k):
        def one(i, carry):
            v, at = i // depth, k * depth + i % depth
            for top in range(0, radial, 8):
                rows = pl.ds(top, 8)
                found = derivative([all_state[m, v, at, rows] for m in range(total)])
                for m in range(total):
                    back[m, v, at, rows] = found[m]
            return carry

        lax.fori_loop(0, comps * depth, one, 0)

    def couple_next(k):
        def one(i, carry):
            v, at = i // depth, k * depth + i % depth
            for top in range(0, radial, 8):
                rows = pl.ds(top, 8)
                pace = step_ref[me * owned + at, rows]
                found = derivative(
                    [
                        all_state[m, v, at, rows]
                        - pace * (all_drive[m, v, at, rows] + back[m, v, at, rows])
                        for m in range(total)
                    ]
                )
                for m in range(total):
                    all_state[m, v, at, rows] = found[m]
            return carry

        lax.fori_loop(0, comps * depth, one, 0)

    load_state = pltpu.make_async_copy(
        start_ref, state.at[:, :, pl.ds(1, layers)], load_sem.at[0]
    )
    load_force = pltpu.make_async_copy(forcing_ref, force, load_sem.at[1])
    for p in range(cycle):
        face_copy(0, p).start()
    load_state.start()
    load_force.start()
    for k in range(chunks):
        begin(0, k)
    load_state.wait()
    exchange(0)
    load_force.wait()
    flux(0)
    for k in range(chunks):
        begin(1, k)
    for k in range(chunks):
        arrived(0, k)
        couple(k)
        begin(2, k)
    for k in range(chunks):
        arrived(1, k)
        couple_next(k)
        begin(3, k)
    for k in range(chunks):
        arrived(2, k)

    def advance(i, carry):
        n, a = i // layers, i % layers
        pace = step_ref[a]
        for v in range(comps):
            state[n, v, a + 1] = state[n, v, a + 1] - pace * (drive[n, v, a] + coupled[n, v, a])
        return carry

    lax.fori_loop(0, instances * layers, advance, 0)
    sent(1)
    exchange(1)
    flux(1)

    def results(k, j):
        here = pl.ds(j * owned + k * depth, depth)
        return (
            pltpu.make_async_copy(
                coupled.at[:, :, here], final_ref.at[:, :, here], out_sem.at[0, k, j]
            ),
            pltpu.make_async_copy(
                drive.at[:, :, here], residual_ref.at[:, :, here], out_sem.at[1, k, j]
            ),
        )

    for k in range(chunks):
        arrived(3, k)

        def finish(i, carry):
            n, j, at = i // owned_now, (i % owned_now) // depth, i % depth
            a = j * owned + k * depth + at
            pace = step_ref[a]
            for v in range(comps):
                rest = drive[n, v, a] + coupled_next[n, v, a]
                drive[n, v, a] = rest
                coupled[n, v, a] = state[n, v, a + 1] - pace * rest
            return carry

        owned_now = parts * depth
        lax.fori_loop(0, instances * owned_now, finish, 0)
        for j in range(parts):
            for copy in results(k, j):
                copy.start()
    for k in range(chunks):
        for j in range(parts):
            for copy in results(k, j):
                copy.wait()
    for phase in (0, 2, 3):
        sent(phase)
    for turn in range(2):
        for p in range(cycle):
            face_copy(turn, p).wait_send()
        for side in range(2):
            edge_copy(turn, side).wait_send()


def local(state_start, forcing, pseudo_step, flux_jacobians, interp_weights, sector_shift):
    instances, comps, layers, radial, width = state_start.shape
    parts, cycle = lax.axis_size("inst"), lax.axis_size("circ")
    owned = layers // parts
    chunks = math.gcd(owned, MOST_CHUNKS)
    row = lax.axis_index("ax")
    turns = jnp.where(row == 1, sector_shift, jnp.mod(cycle - sector_shift, cycle))
    weights = jnp.where(row == 1, jnp.swapaxes(interp_weights, 1, 2), interp_weights)
    block = (instances, comps, layers, radial, width)
    gathered = (instances * parts, comps, owned, radial, width)
    face = (instances, comps, radial, width)
    f32 = jnp.float32
    dma = pltpu.SemaphoreType.DMA
    vmem = pl.BlockSpec(memory_space=pltpu.VMEM)
    smem = pl.BlockSpec(memory_space=pltpu.SMEM)
    hbm = pl.BlockSpec(memory_space=pl.ANY)
    whole = jax.ShapeDtypeStruct(block, f32)
    return pl.pallas_call(
        functools.partial(kernel, (parts, cycle, chunks)),
        out_shape=(whole, whole),
        in_specs=[hbm, hbm, vmem, smem, vmem, smem],
        out_specs=(hbm, hbm),
        scratch_shapes=[
            pltpu.VMEM((instances, comps, layers + 2, radial, width), f32),
            pltpu.VMEM(block, f32),
            pltpu.VMEM(block, f32),
            pltpu.VMEM(gathered, f32),
            pltpu.VMEM(gathered, f32),
            pltpu.VMEM(gathered, f32),
            pltpu.VMEM(block, f32),
            pltpu.VMEM(block, f32),
            pltpu.VMEM((2, cycle) + face, f32),
            pltpu.VMEM((2,) + face, f32),
            pltpu.VMEM((2, 2) + face, f32),
            dma((4, chunks, parts - 1)),
            dma((4, chunks, parts - 1)),
            dma((4, chunks)),
            dma((2, cycle)),
            dma((2, cycle)),
            dma((2, 2)),
            dma((2, 2)),
            dma((2,)),
            dma((2, chunks, parts)),
        ],
        compiler_params=pltpu.CompilerParams(
            collective_id=0, has_side_effects=True, vmem_limit_bytes=56 * 1024 * 1024
        ),
    )(state_start, forcing, pseudo_step, flux_jacobians.reshape(-1) * 0.5, weights, turns)


def solution(mesh):
    cells = P("inst", None, "ax", None, "circ")
    placed = (cells, cells, P("ax", None, "circ"), P(), P("inst", None, None), P("inst"))
    return jax.shard_map(
        local, mesh=mesh, in_specs=placed, out_specs=(cells, cells), check_vma=False
    )
```

time: 903 us -> 473 us (0.52)
  waiting for transfers between devices: 520 us -> 0 us
  Pallas kernels: 0 us -> 459 us
  matrix products: 207 us -> 0 us
  local copies, waits for them, and re-layouts: 142 us -> 9.51 us
  between operations: 14.5 us -> 0.66 us
  starting transfers between devices: 10.7 us -> 0 us
    all_gather x2 -> x0, waiting for transfers between devices: 515 us -> none  [local(): lax.all_gather(state, 'inst', axis=0, tiled=True)]
    pallas_call x0 -> x1, Pallas kernels: none -> 459 us  [local(): pl.pallas_call(functools.partial(kernel, (parts, cycle, chunks)), out_sha...]
    dot_general x10 -> x0, matrix products: 207 us -> none  [the longest x6 155 us: directional(): jnp.einsum('vw,iwarc->ivarc', jacobian, central, precision=lax.Precision....]
    slice x10 -> x0, local copies, waits for them, and re-layouts: 75.9 us -> none  [the longest x3 31.5 us: with_halo(): lax.slice_in_dim(cells, cells.shape[dim] - width, cells.shape[dim], axis=...]
    ppermute x4 -> x0, local copies, waits for them, and re-layouts: 30.3 us -> none  [the longest x2 15.1 us: with_halo(): lax.ppermute(tail, axis, [(i, (i + 1) % count) for i in range(count)])]
    unnamed x24 -> x5, local copies, waits for them, and re-layouts: 28.4 us -> 8.9 us
    ppermute x10 -> x0, starting transfers between devices: 10.6 us -> none  [the longest x4 4.27 us: from_behind(): return lax.ppermute(block, axis, route)]
  transfers between devices with their start and end apart: 12 -> 0, of which waited for: 3 -> 0; matrix products, arithmetic and copies ran while one was open for 20% -> 0% of each run, Pallas kernels for 0% -> 0%
where the time goes in v1:
time: 473 us
  Pallas kernels  459 us (97%)
  local copies, waits for them, and re-layouts  9.51 us (2%)
    pallas_call x1, Pallas kernels, local(): pl.pallas_call(functools.partial(kernel, (parts, cycle, chunks)), out_sha...  459 us

profile of v1, /device:TPU:8, one launch (start us, length us, event | category | flops | bytes accessed | tf_op | source)
XLA Modules:
  0.0 473.2 jit_solution(1716537985803206787)
XLA Ops:
  0.6 1.2 broadcast_select_fusion.turn_ref
  1.9 0.7 broadcast_multiply_fusion
  2.6 0.6 mul.10.jac_ref
  3.2 1.1 copy.11
  4.3 1.7 bitcast_select_fusion.weights_ref
  6.0 459.3 %shard_map.77 = (f32[4,5,32,16,128]{4,3,2,1,0:T(8,128)}, f32[4,5,32,16,128]{4,3,2,1,0:T(8,128)}) custom-call(f32[4,5,32,16,128]{4,3,2,1,0:T(8,128)} %start_ref.1, f32[4,5,32,16,128]{4,3,2,1,0:T(8,128)} %forcing_ref.1, f32[32,16,128]{2,1,0:T(8,128)} %step_ref.1, f32[75]{0:T(128)} %mul.10.jac_ref, f32[4,128,128]{2,1,0:T(8,128)} %bitcast_select_fusion.weights_ref, ...), custom_call_target="tpu_custom_call" | custom-call | tf_op jit(solution)/shard_map/pallas_call | solution.py:331
  465.3 0.0 copy-start
  465.3 5.5 %copy.14 = f32[4,5,32,16,128]{4,3,2,1,0:T(8,128)} copy(f32[4,5,32,16,128]{4,3,2,1,0:T(8,128)} %get-tuple-element.4) | data formatting | bytes 10485760
  470.8 0.0 copy-done
  470.8 2.4 copy.15
  (1 shorter events, 0.0 us)
Async XLA Ops:
  465.3 5.5 %copy-start = (f32[4,5,32,16,128]{4,3,2,1,0:T(8,128)S(1)}, f32[4,5,32,16,128]{4,3,2,1,0:T(8,128)}, u32[]{:S(2)}) copy-start(f32[4,5,32,16,128]{4,3,2,1,0:T(8,128)} %get-tuple-element.5) | copy-start | bytes 15728644

commit v2 on v1

--- a/solution.py
+++ b/solution.py
@@ -36,11 +36,11 @@
 
 def kernel(
     sizes,
-    start_ref, forcing_ref, step_ref, jac_ref, weights_ref, turn_ref,
-    final_ref, residual_ref,
-    state, force, drive, all_state, all_drive, back, coupled, coupled_next,
+    start_ref, forcing_ref, step_ref, jac_ref, weights_ref, shift_ref,
+    coupled, drive,
+    state, force, all_state, all_drive, back, coupled_next,
     faces, edges, edges_in,
-    z_send, z_recv, z_local, f_send, f_recv, e_send, e_recv, load_sem, out_sem,
+    z_send, z_recv, z_local, f_send, f_recv, e_send, e_recv, load_sem,
 ):
     parts, cycle, chunks = sizes
     instances, comps, layers, radial, width = drive.shape
@@ -136,6 +136,14 @@
     lane = lax.broadcasted_iota(jnp.int32, (radial, width), 1)
     line = lax.broadcasted_iota(jnp.int32, (radial, width), 0)
 
+    def turned(n):
+        shift = shift_ref[n]
+        return jnp.where(row == 1, shift, lax.rem(cycle - shift, cycle))
+
+    def blend(n):
+        weights = weights_ref[n]
+        return jnp.where(row == 1, weights.T, weights)
+
     def exchange(turn):
         for p in range(cycle):
             if turn == 1:
@@ -157,12 +165,12 @@
         for p in range(cycle):
             face_copy(turn, p).wait_recv()
         for n in range(instances):
-            taken = jnp.full((comps, radial, width), turn_ref[n], jnp.int32)
+            taken = jnp.full((comps, radial, width), turned(n), jnp.int32)
             facing = faces[turn, 0, n]
             for p in range(1, cycle):
                 facing = jnp.where(taken == p, faces[turn, p, n], facing)
             ghost = jnp.dot(
-                facing.reshape(comps * radial, width), weights_ref[n],
+                facing.reshape(comps * radial, width), blend(n),
                 precision=HIGHEST, preferred_element_type=jnp.float32,
             ).reshape(comps, radial, width)
             empty = jnp.zeros_like(ghost)
@@ -193,7 +201,7 @@
                 value = curves[v] - force[n, v, a]
                 for d in range(3):
                     for w in range(comps):
-                        value = value + jac_ref[(d * comps + v) * comps + w] * rises[d][w]
+                        value = value + (0.5 * jac_ref[d, v, w]) * rises[d][w]
                 drive[n, v, a] = value
             return carry
 
@@ -269,17 +277,6 @@
     exchange(1)
     flux(1)
 
-    def results(k, j):
-        here = pl.ds(j * owned + k * depth, depth)
-        return (
-            pltpu.make_async_copy(
-                coupled.at[:, :, here], final_ref.at[:, :, here], out_sem.at[0, k, j]
-            ),
-            pltpu.make_async_copy(
-                drive.at[:, :, here], residual_ref.at[:, :, here], out_sem.at[1, k, j]
-            ),
-        )
-
     for k in range(chunks):
         arrived(3, k)
 
@@ -295,13 +292,6 @@
 
         owned_now = parts * depth
         lax.fori_loop(0, instances * owned_now, finish, 0)
-        for j in range(parts):
-            for copy in results(k, j):
-                copy.start()
-    for k in range(chunks):
-        for j in range(parts):
-            for copy in results(k, j):
-                copy.wait()
     for phase in (0, 2, 3):
         sent(phase)
     for turn in range(2):
@@ -316,9 +306,6 @@
     parts, cycle = lax.axis_size("inst"), lax.axis_size("circ")
     owned = layers // parts
     chunks = math.gcd(owned, MOST_CHUNKS)
-    row = lax.axis_index("ax")
-    turns = jnp.where(row == 1, sector_shift, jnp.mod(cycle - sector_shift, cycle))
-    weights = jnp.where(row == 1, jnp.swapaxes(interp_weights, 1, 2), interp_weights)
     block = (instances, comps, layers, radial, width)
     gathered = (instances * parts, comps, owned, radial, width)
     face = (instances, comps, radial, width)
@@ -330,17 +317,15 @@
     whole = jax.ShapeDtypeStruct(block, f32)
     return pl.pallas_call(
         functools.partial(kernel, (parts, cycle, chunks)),
-        out_shape=(whole, whole),
+        out_shape=(pltpu.VMEM(block, f32), pltpu.VMEM(block, f32)),
         in_specs=[hbm, hbm, vmem, smem, vmem, smem],
-        out_specs=(hbm, hbm),
+        out_specs=(vmem, vmem),
         scratch_shapes=[
             pltpu.VMEM((instances, comps, layers + 2, radial, width), f32),
-            pltpu.VMEM(block, f32),
             pltpu.VMEM(block, f32),
             pltpu.VMEM(gathered, f32),
             pltpu.VMEM(gathered, f32),
             pltpu.VMEM(gathered, f32),
-            pltpu.VMEM(block, f32),
             pltpu.VMEM(block, f32),
             pltpu.VMEM((2, cycle) + face, f32),
             pltpu.VMEM((2,) + face, f32),
@@ -353,12 +338,11 @@
             dma((2, 2)),
             dma((2, 2)),
             dma((2,)),
-            dma((2, chunks, parts)),
         ],
         compiler_params=pltpu.CompilerParams(
-            collective_id=0, has_side_effects=True, vmem_limit_bytes=56 * 1024 * 1024
+            collective_id=0, has_side_effects=True, vmem_limit_bytes=42 * 1024 * 1024
         ),
-    )(state_start, forcing, pseudo_step, flux_jacobians.reshape(-1) * 0.5, weights, turns)
+    )(state_start, forcing, pseudo_step, flux_jacobians, interp_weights, sector_shift)
 
 
 def solution(mesh):

time: 473 us -> 467 us (0.987)
  no operation moved by 1% of the time
where the time goes in v2:
time: 467 us
  Pallas kernels  458 us (98%)
  local copies, waits for them, and re-layouts  7.98 us (2%)
    pallas_call x1, Pallas kernels, local(): pl.pallas_call(functools.partial(kernel, (parts, cycle, chunks)), out_sha...  458 us

profile of v2, /device:TPU:8, one launch (start us, length us, event | category | flops | bytes accessed | tf_op | source)
XLA Modules:
  0.0 466.8 jit_solution(7313497090353384076)
XLA Ops:
  0.6 0.7 copy.8.jac_ref
  1.3 0.0 copy-start
  1.3 0.9 copy-done
  2.3 0.0 copy-start.1
  2.3 0.9 copy-done.1
  3.2 0.0 copy-start.2
  3.2 0.7 copy-done.2
  3.9 458.1 %shard_map.77 = (f32[4,5,32,16,128]{4,3,2,1,0:T(8,128)S(1)}, f32[4,5,32,16,128]{4,3,2,1,0:T(8,128)S(1)}) custom-call(f32[4,5,32,16,128]{4,3,2,1,0:T(8,128)} %start_ref.1, f32[4,5,32,16,128]{4,3,2,1,0:T(8,128)} %forcing_ref.1, f32[32,16,128]{2,1,0:T(8,128)S(1)} %copy-done, f32[3,5,5]{2,1,0:T(8,128)S(1)} %copy.8.jac_ref, f32[4,128,128]{2,1,0:T(8,128)S(1)} %copy-done.1, ...), custom_call_target="tpu_custom_call" | custom-call | tf_op jit(solution)/shard_map/pallas_call | solution.py:318
  462.0 2.4 copy.11
  464.4 2.4 copy.12
Async XLA Ops:
  1.3 0.9 copy-start
  2.3 0.9 copy-start.1
  3.2 0.7 copy-start.2

commit v3 on v2

--- a/solution.py
+++ b/solution.py
@@ -36,10 +36,10 @@
 
 def kernel(
     sizes,
-    start_ref, forcing_ref, step_ref, jac_ref, weights_ref, shift_ref,
+    start_ref, forcing_ref, step_whole, jac_ref, weights_whole, shift_ref,
     coupled, drive,
     state, force, all_state, all_drive, back, coupled_next,
-    faces, edges, edges_in,
+    faces, edges, edges_in, step_ref, weights_ref,
     z_send, z_recv, z_local, f_send, f_recv, e_send, e_recv, load_sem,
 ):
     parts, cycle, chunks = sizes
@@ -242,13 +242,19 @@
         start_ref, state.at[:, :, pl.ds(1, layers)], load_sem.at[0]
     )
     load_force = pltpu.make_async_copy(forcing_ref, force, load_sem.at[1])
+    load_step = pltpu.make_async_copy(step_whole, step_ref, load_sem.at[2])
+    load_weights = pltpu.make_async_copy(weights_whole, weights_ref, load_sem.at[3])
     for p in range(cycle):
         face_copy(0, p).start()
     load_state.start()
+    load_weights.start()
+    load_step.start()
     load_force.start()
     for k in range(chunks):
         begin(0, k)
     load_state.wait()
+    load_weights.wait()
+    load_step.wait()
     exchange(0)
     load_force.wait()
     flux(0)
@@ -313,12 +319,12 @@
     dma = pltpu.SemaphoreType.DMA
     vmem = pl.BlockSpec(memory_space=pltpu.VMEM)
     smem = pl.BlockSpec(memory_space=pltpu.SMEM)
-    hbm = pl.BlockSpec(memory_space=pl.ANY)
+    hbm = pl.BlockSpec(memory_space=pltpu.HBM)
     whole = jax.ShapeDtypeStruct(block, f32)
     return pl.pallas_call(
         functools.partial(kernel, (parts, cycle, chunks)),
         out_shape=(pltpu.VMEM(block, f32), pltpu.VMEM(block, f32)),
-        in_specs=[hbm, hbm, vmem, smem, vmem, smem],
+        in_specs=[hbm, hbm, hbm, smem, hbm, smem],
         out_specs=(vmem, vmem),
         scratch_shapes=[
             pltpu.VMEM((instances, comps, layers + 2, radial, width), f32),
@@ -330,6 +336,8 @@
             pltpu.VMEM((2, cycle) + face, f32),
             pltpu.VMEM((2,) + face, f32),
             pltpu.VMEM((2, 2) + face, f32),
+            pltpu.VMEM(pseudo_step.shape, f32),
+            pltpu.VMEM(interp_weights.shape, f32),
             dma((4, chunks, parts - 1)),
             dma((4, chunks, parts - 1)),
             dma((4, chunks)),
@@ -337,10 +345,10 @@
             dma((2, cycle)),
             dma((2, 2)),
             dma((2, 2)),
-            dma((2,)),
+            dma((4,)),
         ],
         compiler_params=pltpu.CompilerParams(
-            collective_id=0, has_side_effects=True, vmem_limit_bytes=42 * 1024 * 1024
+            collective_id=0, has_side_effects=True, vmem_limit_bytes=50 * 1024 * 1024 + 384 * 1024
         ),
     )(state_start, forcing, pseudo_step, flux_jacobians, interp_weights, sector_shift)
 

time: 467 us -> 465 us (level)
  no operation moved by 1% of the time
where the time goes in v3:
time: 465 us
  Pallas kernels  458 us (98%)
  local copies, waits for them, and re-layouts  6.02 us (1%)
    pallas_call x1, Pallas kernels, local(): pl.pallas_call(functools.partial(kernel, (parts, cycle, chunks)), out_sha...  458 us

profile of v3, /device:TPU:8, one launch (start us, length us, event | category | flops | bytes accessed | tf_op | source)
XLA Modules:
  0.0 465.0 jit_solution(4030582619386070987)
XLA Ops:
  0.6 1.3 copy.8.jac_ref
  1.9 458.3 %shard_map.77 = (f32[4,5,32,16,128]{4,3,2,1,0:T(8,128)S(1)}, f32[4,5,32,16,128]{4,3,2,1,0:T(8,128)S(1)}) custom-call(f32[4,5,32,16,128]{4,3,2,1,0:T(8,128)} %start_ref.1, f32[4,5,32,16,128]{4,3,2,1,0:T(8,128)} %forcing_ref.1, f32[32,16,128]{2,1,0:T(8,128)} %step_whole.1, f32[3,5,5]{2,1,0:T(8,128)} %copy.8.jac_ref, f32[4,128,128]{2,1,0:T(8,128)} %weights_whole.1, ...), custom_call_target="tpu_custom_call" | custom-call | tf_op jit(solution)/shard_map/pallas_call | solution.py:324
  460.2 2.4 copy.11
  462.6 2.4 copy.12
